TPU v7x, 256 devices: a whole 4x4x8 slice. The times are simulated.
256 devices in a mesh: ctx: 32 (over y, z), head: 8 (over x, core).
Axes of the slice: x: 4, y: 4, z: 8, core: 2. Of those that a mesh axis runs over, the one named last changes fastest.
Arguments:
- tokens: bfloat16 [65536, 2048], P('ctx'), may hold values from -6 to 6
- w_query: bfloat16 [2048, 2048], P(None, 'head'), may hold values from -0.125 to 0.125
- w_key: bfloat16 [2048, 2048], P(None, 'head'), may hold values from -0.125 to 0.125
- w_value: bfloat16 [2048, 2048], P(None, 'head'), may hold values from -0.125 to 0.125
- w_out: bfloat16 [2048, 2048], P('head'), may hold values from -0.125 to 0.125
- decay_rate: float32 [65536, 16], P('ctx', 'head'), may hold values from 0 to 1
- level_row_index: int32 [65536], P('ctx'), may hold values from 0 to 63
- level_weight_table: float32 [64, 16, 11], P(None, 'head'), may hold values from 0.2 to 2
Outputs:
- mixed: bfloat16 [65536, 2048], P('ctx', 'head')
All inputs are finite; a program needn't handle non-finite values.
Results may differ from a plain program's by a relative error of at most 0.02.
Values may be sent and summed in bfloat16 or wider, within the bound.
A program may use at most 128 MiB of HBM per device.

v0:
```python
import functools

import jax
import jax.numpy as jnp
from jax import lax
from jax.experimental import pallas as pl
from jax.experimental.pallas import tpu as pltpu
from jax.sharding import PartitionSpec as P

F32, BF16 = jnp.float32, jnp.bfloat16
MESH = pl.DeviceIdType.MESH
EPSILON = 1e-06
DH = 128
HEADS = 2
CHUNK = 256
CHUNKS = 8
HALF = CHUNKS // 2
LOCAL = 3
CTX_Z, CTX_Y = 3, 2
CROSS = CTX_Z + CTX_Y
FIRST_LOCAL, FIRST_CROSS = 3, 6
ROWS = 16
CUM, KDEC = 11, 12
MSG = DH + 16


def dot(a, b, dims=((1,), (0,))):
    return lax.dot_general(a, b, (dims, ((), ())), preferred_element_type=F32)


def split(x, terms):
    parts = []
    for _ in range(terms):
        part = x.astype(BF16)
        parts.append(part)
        x = x - part.astype(F32)
    return parts


def mirror(index, bits):
    size = 2**bits
    low = lax.rem(index, size)
    return index - low + (size - 1 - low)


def kernel(
    tokens, w_query, w_key, w_value, w_out, rates, row_index, table,
    out,
    tok, wkv, wq, kv, states, local_states, local_out, cross_lhs, cross_states,
    table_rows, rate_rows, cum_rows, cols, send_state, recv_state,
    gathered, other, weights, spare, staged,
    tok_sem, w_sem, wl_sem, ws_send, ws_recv, wx_send, wx_recv,
    st_send, st_recv, g_send, g_recv,
):
    pos = lax.axis_index("ctx")
    me = lax.axis_index("head")
    x = lax.div(me, 2)
    core = lax.rem(me, 2)
    pair = x + 1 - 2 * lax.rem(x, 2)
    across = 3 - x
    far = lax.rem(x + 2, 4)
    z = lax.rem(pos, 2**CTX_Z)
    y = lax.div(pos, 2**CTX_Z)
    sibling_id = (pos, 2 * x + 1 - core)
    pair_id = (pos, 2 * pair + core)
    across_id = (pos, 2 * across + core)
    far_id = (pos, 2 * far + core)
    ctx_ids = [(y * 2**CTX_Z + mirror(z, b + 1), me) for b in range(CTX_Z)]
    ctx_ids += [(mirror(y, b + 1) * 2**CTX_Z + z, me) for b in range(CTX_Y)]
    partners = [sibling_id, pair_id, across_id, far_id] + ctx_ids

    barrier = pltpu.get_barrier_semaphore()
    for partner in partners:
        pl.semaphore_signal(barrier, inc=1, device_id=partner, device_id_type=MESH)

    def weight_copy(source, head, part):
        return pltpu.make_async_copy(
            source.at[:, pl.ds(head * DH, DH)],
            wkv.at[head, :, pl.ds(part * DH, DH)],
            w_sem.at[head * 2 + part],
        )

    def token_copy(u):
        return pltpu.make_async_copy(
            tokens.at[pl.ds(pl.multiple_of(u * CHUNK, CHUNK), CHUNK), :], tok.at[u], tok_sem.at[u]
        )

    query_copy = pltpu.make_async_copy(w_query, wq, w_sem.at[4])
    weight_copy(w_key, 0, 0).start()
    weight_copy(w_value, 0, 1).start()
    for u in range(CHUNKS):
        token_copy(u).start()
        if u == 2:
            weight_copy(w_key, 1, 0).start()
            weight_copy(w_value, 1, 1).start()
    query_copy.start()

    homes = [(weights, 0, 0, x), (weights, 0, 1, across), (spare, None, 0, far), (spare, None, 1, pair)]

    def piece(buffer, slot, a, k):
        view = buffer.at[slot, a] if slot is not None else buffer.at[a]
        return view.at[pl.ds(k * 256, 256), :]

    own_pieces, sibling_pieces = [], []
    for i, (buffer, slot, a, chip) in enumerate(homes):
        columns = pl.ds(pl.multiple_of((2 * chip + core) * 256, 256), 256)
        own_pieces.append(
            pltpu.make_async_copy(w_out.at[:, columns], piece(buffer, slot, a, 0), wl_sem.at[i])
        )
        columns = pl.ds(pl.multiple_of((2 * chip + 1 - core) * 256, 256), 256)
        sibling_pieces.append(
            pltpu.make_async_remote_copy(
                src_ref=w_out.at[:, columns],
                dst_ref=piece(buffer, slot, a, 1),
                send_sem=ws_send.at[i],
                recv_sem=ws_recv.at[i],
                device_id=sibling_id,
                device_id_type=MESH,
            )
        )
        own_pieces[-1].start()

    def weight_send(i, source, slot, target):
        return pltpu.make_async_remote_copy(
            src_ref=source, dst_ref=weights.at[slot], send_sem=wx_send.at[i],
            recv_sem=wx_recv.at[i], device_id=target, device_id_type=MESH,
        )

    weight_sends = [
        weight_send(0, weights.at[0], 2, across_id),
        weight_send(1, spare, 1, pair_id),
        weight_send(2, spare, 3, far_id),
    ]

    for u in range(CHUNKS):
        rate_rows[HEADS * u : HEADS * (u + 1), :] = rates[:, u * CHUNK : (u + 1) * CHUNK]
    before = lax.broadcasted_iota(jnp.int32, (CHUNK, CHUNK), 0)
    after = lax.broadcasted_iota(jnp.int32, (CHUNK, CHUNK), 1)
    upper = (before <= after).astype(BF16)
    cum = sum(dot(part, upper) for part in split(-rate_rows[...], 3))
    cum_rows[...] = cum
    last = cum[:, CHUNK - 1 :]
    key_decay = jnp.exp(last - cum)
    totals = [[last[HEADS * u + h : HEADS * u + h + 1, :] for u in range(CHUNKS)] for h in range(HEADS)]

    table_rows[...] = jnp.zeros_like(table_rows)
    levels = table.shape[0]
    for h in range(HEADS):
        table_rows[h * ROWS : h * ROWS + levels, :] = table[:, h, :]
    slots = table.shape[2]
    parts = split(table_rows[...], 3)
    level = lax.broadcasted_iota(jnp.int32, (ROWS, 1), 0)
    for u in range(CHUNKS):
        span = slice(u * CHUNK, (u + 1) * CHUNK)
        chosen = lax.broadcasted_iota(jnp.int32, (slots, CHUNK), 0) == row_index[:, span]
        chosen = jnp.where(chosen, 1.0, 0.0).astype(BF16)
        mix = sum(dot(part, chosen) for part in parts)
        rows = []
        for h in range(HEADS):
            none = jnp.zeros((1, 1), F32)
            offsets = [
                none,
                totals[h][u - 1] if u % 2 else none,
                sum(totals[h][4:u], none),
                sum(totals[h][:u], none),
            ]
            offset = jnp.where(level == 4, offsets[1], offsets[0])
            offset = jnp.where(level == 5, offsets[2], offset)
            offset = jnp.where(level >= FIRST_CROSS, offsets[3], offset)
            here = HEADS * u + h
            cum_row = cum[here : here + 1, :]
            factor = jnp.exp(jnp.where(level >= FIRST_LOCAL, cum_row + offset, 0.0))
            for bit in range(LOCAL):
                if not (u >> bit) & 1:
                    factor = jnp.where(level == FIRST_LOCAL + bit, 0.0, factor)
            table_of_rows = mix[h * ROWS : (h + 1) * ROWS, :] * factor
            table_of_rows = jnp.where(level == CUM, cum_row, table_of_rows)
            table_of_rows = jnp.where(level == KDEC, key_decay[here : here + 1, :], table_of_rows)
            rows.append(table_of_rows)
        cols[u, :, 0 : HEADS * ROWS] = jnp.concatenate(rows, axis=0).T

    pl.semaphore_wait(barrier, len(partners))
    for copy in sibling_pieces:
        copy.start()

    def key_value(h, u):
        result = dot(tok[u], wkv[h]).astype(BF16)
        kv[h, u] = result
        decay = cols[u, :, pl.ds(h * ROWS + KDEC, 1)]
        decayed = (result[:, :DH].astype(F32) * decay).astype(BF16)
        states[h, u] = dot(decayed, result[:, DH:], ((0,), (0,)))

    def merge(first, second):
        return jnp.exp(second[1]) * first[0] + second[0], first[1] + second[1]

    running = [None] * HEADS
    passed = [jnp.zeros((1, 1), F32) for _ in range(HEADS)]

    def state_copy(h, b):
        return pltpu.make_async_remote_copy(
            src_ref=send_state.at[h, b], dst_ref=recv_state.at[h, b], send_sem=st_send.at[h, b],
            recv_sem=st_recv.at[h, b], device_id=ctx_ids[b], device_id_type=MESH,
        )

    def send(h, b):
        state, total = running[h]
        send_state[h, b, 0:DH, :] = state.astype(BF16)
        row = lax.broadcasted_iota(jnp.int32, (16, DH), 0)
        tail = jnp.zeros((16, DH), F32)
        for i, part in enumerate(split(total, 3)):
            tail = jnp.where(row == i, part.astype(F32), tail)
        send_state[h, b, DH:MSG, :] = tail.astype(BF16)
        state_copy(h, b).start()

    def receive(h, b):
        state_copy(h, b).wait_recv()
        there = recv_state[h, b, 0:DH, :].astype(F32)
        tail = recv_state[h, b, DH:MSG, :].astype(F32)
        there_total = tail[0:1, 0:1] + tail[1:2, 0:1] + tail[2:3, 0:1]
        is_upper = lax.rem(lax.div(pos, 2**b), 2) == 1
        cross = jnp.where(is_upper, jnp.exp(passed[h]) * there, 0.0)
        cross_states[h, b * DH : (b + 1) * DH, :] = cross.astype(BF16)
        state, total = running[h]
        passed[h] = passed[h] + jnp.where(is_upper, there_total, 0.0)
        low = jnp.where(is_upper, there, state)
        high = jnp.where(is_upper, state, there)
        high_total = jnp.where(is_upper, total, there_total)
        running[h] = (jnp.exp(high_total) * low + high, total + there_total)
        if b + 1 < CROSS:
            send(h, b + 1)

    def own_state(h):
        single = [(states[h, u], totals[h][u]) for u in range(CHUNKS)]
        pairs = [merge(single[2 * i], single[2 * i + 1]) for i in range(4)]
        quads = [merge(pairs[2 * i], pairs[2 * i + 1]) for i in range(2)]
        running[h] = merge(quads[0], quads[1])
        send(h, 0)
        zero = jnp.zeros((DH, DH), BF16)
        for u in range(CHUNKS):
            lower = [
                single[u - 1][0].astype(BF16) if u & 1 else zero,
                pairs[u // 2 - 1][0].astype(BF16) if u & 2 else zero,
                quads[0][0].astype(BF16) if u & 4 else zero,
            ]
            for i, state in enumerate(lower):
                local_states[h, u, i * DH : (i + 1) * DH, :] = state

    weight_copy(w_key, 0, 0).wait()
    weight_copy(w_value, 0, 1).wait()

    def first_head(u, carry):
        token_copy(u).wait()
        key_value(0, u)
        return carry

    lax.fori_loop(0, CHUNKS, first_head, 0)
    own_state(0)

    for copy in own_pieces:
        copy.wait()
    for copy in sibling_pieces:
        copy.wait_recv()
    for copy in weight_sends:
        copy.start()

    weight_copy(w_key, 1, 0).wait()
    weight_copy(w_value, 1, 1).wait()

    def second_head(u, carry):
        key_value(1, u)
        return carry

    lax.fori_loop(0, CHUNKS, second_head, 0)
    own_state(1)
    receive(0, 0)
    query_copy.wait()

    def local_part(u, carry):
        queries = dot(tok[u], wq[...]).astype(BF16)
        token = lax.broadcasted_iota(jnp.int32, (CHUNK, CHUNK), 0)
        source = lax.broadcasted_iota(jnp.int32, (CHUNK, CHUNK), 1)
        causal = token >= source
        same_block = lax.div(token, 64) == lax.div(source, 64)
        same_pair = lax.div(token, 128) == lax.div(source, 128)
        for h in range(HEADS):
            column = lambda row: cols[u, :, pl.ds(h * ROWS + row, 1)]
            query = queries[:, h * DH : (h + 1) * DH]
            key, value = kv[h, u, :, 0:DH], kv[h, u, :, DH : 2 * DH]
            gap = column(CUM) - cum_rows[pl.ds(HEADS * u + h, 1), :]
            decay = jnp.exp(jnp.where(causal, gap, -1e30))
            mix = jnp.where(same_block, column(0), jnp.where(same_pair, column(1), column(2)))
            scores = dot(query, key, ((1,), (1,)))
            result = dot((scores * decay * mix).astype(BF16), value)
            query = query.astype(F32)
            lhs = [(query * column(FIRST_LOCAL + i)).astype(BF16) for i in range(LOCAL)]
            result += dot(jnp.concatenate(lhs, axis=1), local_states[h, u])
            local_out[u, :, h * DH : (h + 1) * DH] = result
            for i in range(CROSS):
                cross_lhs[u, h, :, i * DH : (i + 1) * DH] = (
                    query * column(FIRST_CROSS + i)
                ).astype(BF16)
        return carry

    lax.fori_loop(0, 3, local_part, 0)
    receive(1, 0)
    receive(0, 1)
    lax.fori_loop(3, 6, local_part, 0)
    receive(1, 1)
    receive(0, 2)
    lax.fori_loop(6, CHUNKS, local_part, 0)
    receive(1, 2)
    receive(0, 3)
    receive(1, 3)
    receive(0, 4)
    receive(1, 4)

    mine = lax.div(x, 2)

    def moved(kind, j, source, target_slot, target):
        return pltpu.make_async_remote_copy(
            src_ref=source, dst_ref=slot(j, target_slot), send_sem=g_send.at[kind, j],
            recv_sem=g_recv.at[kind, j], device_id=target, device_id_type=MESH,
        )

    def slot(j, number):
        return gathered.at[j, :, pl.ds(number * 256, 256)]

    def own_to_sibling(j):
        return moved(0, j, slot(j, 0), 1, sibling_id)

    def own_to_pair(j):
        return moved(1, j, slot(j, 0), 2, pair_id)

    def pair_to_sibling(j):
        return moved(2, j, slot(j, 2), 3, sibling_id)

    def other_to_across(j):
        return moved(3, j, other.at[j], 4, across_id)

    def across_to_sibling(j):
        return moved(4, j, slot(j, 4), 5, sibling_id)

    def across_to_pair(j):
        return moved(5, j, slot(j, 4), 6, pair_id)

    def far_to_sibling(j):
        return moved(6, j, slot(j, 6), 7, sibling_id)

    def mine_rows(j):
        return pl.ds(pl.multiple_of((mine * HALF + j) * CHUNK, CHUNK), CHUNK)

    def result_to_across(j):
        return pltpu.make_async_remote_copy(
            src_ref=staged.at[j], dst_ref=out.at[mine_rows(j), :], send_sem=g_send.at[7, j],
            recv_sem=g_recv.at[7, j], device_id=across_id, device_id_type=MESH,
        )

    def normed(u):
        heads = []
        for h in range(HEADS):
            value = local_out[u, :, h * DH : (h + 1) * DH] + dot(cross_lhs[u, h], cross_states[h])
            square = jnp.mean(value * value, axis=1, keepdims=True)
            heads.append((value * lax.rsqrt(square + EPSILON)).astype(BF16))
        return jnp.concatenate(heads, axis=1)

    def finish(j, carry):
        other[j] = normed((1 - mine) * HALF + j)
        other_to_across(j).start()
        gathered[j, :, 0:256] = normed(mine * HALF + j)
        own_to_pair(j).start()
        own_to_sibling(j).start()
        return carry

    lax.fori_loop(0, HALF, finish, 0)

    def forward(j, carry):
        other_to_across(j).wait_recv()
        across_to_pair(j).start()
        across_to_sibling(j).start()
        own_to_pair(j).wait_recv()
        pair_to_sibling(j).start()
        return carry

    lax.fori_loop(0, HALF, forward, 0)
    for copy in weight_sends:
        copy.wait_recv()

    for_own, for_across = (0, 1, 1, 0), (1, 0, 0, 1)

    def project(j, carry):
        across_to_pair(j).wait_recv()
        far_to_sibling(j).start()
        own_to_sibling(j).wait_recv()
        pair_to_sibling(j).wait_recv()
        across_to_sibling(j).wait_recv()

        def product(a, r):
            return dot(gathered[j, :, r * 512 : (r + 1) * 512], weights[r, a[r]])

        to_across = product(for_across, 0) + product(for_across, 1) + product(for_across, 2)
        to_own = product(for_own, 0) + product(for_own, 1) + product(for_own, 2)
        far_to_sibling(j).wait_recv()
        staged[j] = (to_across + product(for_across, 3)).astype(BF16)
        result_to_across(j).start()
        out[mine_rows(j), :] = (to_own + product(for_own, 3)).astype(BF16)
        return carry

    lax.fori_loop(0, HALF, project, 0)

    def drain(j, carry):
        for copy in (
            own_to_sibling, own_to_pair, pair_to_sibling, other_to_across,
            across_to_sibling, across_to_pair, far_to_sibling,
        ):
            copy(j).wait_send()
        result_to_across(j).wait()
        return carry

    lax.fori_loop(0, HALF, drain, 0)
    for copy in sibling_pieces + weight_sends:
        copy.wait_send()
    for h in range(HEADS):
        for b in range(CROSS):
            state_copy(h, b).wait_send()


def shards(tokens, w_query, w_key, w_value, w_out, decay_rate, level_row_index, level_weight_table):
    rows, depth = tokens.shape
    width = w_query.shape[1]
    vmem = functools.partial(pltpu.VMEM)
    dma = pltpu.SemaphoreType.DMA
    hbm, on_chip = pl.BlockSpec(memory_space=pl.ANY), pl.BlockSpec(memory_space=pltpu.VMEM)
    call = pl.pallas_call(
        kernel,
        out_shape=jax.ShapeDtypeStruct((rows, width), BF16),
        in_specs=[hbm] * 5 + [on_chip] * 3,
        out_specs=on_chip,
        scratch_shapes=[
            vmem((CHUNKS, CHUNK, depth), BF16),
            vmem((HEADS, depth, 2 * DH), BF16),
            vmem((depth, width), BF16),
            vmem((HEADS, CHUNKS, CHUNK, 2 * DH), BF16),
            vmem((HEADS, CHUNKS, DH, DH), F32),
            vmem((HEADS, CHUNKS, LOCAL * DH, DH), BF16),
            vmem((CHUNKS, CHUNK, width), F32),
            vmem((CHUNKS, HEADS, CHUNK, CROSS * DH), BF16),
            vmem((HEADS, CROSS * DH, DH), BF16),
            vmem((HEADS * ROWS, level_weight_table.shape[0]), F32),
            vmem((HEADS * CHUNKS, CHUNK), F32),
            vmem((HEADS * CHUNKS, CHUNK), F32),
            vmem((CHUNKS, CHUNK, 128), F32),
            vmem((HEADS, CROSS, MSG, DH), BF16),
            vmem((HEADS, CROSS, MSG, DH), BF16),
            vmem((HALF, CHUNK, 8 * width), BF16),
            vmem((HALF, CHUNK, width), BF16),
            vmem((4, 2, 2 * width, width), BF16),
            vmem((2, 2 * width, width), BF16),
            vmem((HALF, CHUNK, width), BF16),
            dma((CHUNKS,)), dma((5,)), dma((4,)), dma((4,)), dma((4,)), dma((3,)), dma((3,)),
            dma((HEADS, CROSS)), dma((HEADS, CROSS)), dma((8, HALF)), dma((8, HALF)),
        ],
        compiler_params=pltpu.CompilerParams(
            collective_id=0, has_side_effects=True, vmem_limit_bytes=56 * 2**20
        ),
    )
    return call(
        tokens, w_query, w_key, w_value, w_out, decay_rate.T, level_row_index.reshape(1, rows),
        level_weight_table.transpose(2, 1, 0),
    )


def solution(mesh):
    placed = (
        P("ctx", None),
        P(None, "head"),
        P(None, "head"),
        P(None, "head"),
        P("head", None),
        P("ctx", "head"),
        P("ctx"),
        P(None, "head", None),
    )
    return jax.shard_map(
        shards, mesh=mesh, in_specs=placed, out_specs=P("ctx", "head"), check_vma=False
    )
```

profile of v0, /device:TPU:1, one launch (start us, length us, event | category | flops | bytes accessed | tf_op | source)
XLA Modules:
  0.0 77.2 jit_solution(1651863967814452164)
XLA Ops:
  0.0 75.0 %shard_map.82 = bf16[2048,256]{1,0:T(8,128)(2,1)} custom-call(bf16[2048,2048]{1,0:T(8,128)(2,1)} %tokens.1, bf16[2048,256]{1,0:T(8,128)(2,1)} %w_query.1, bf16[2048,256]{1,0:T(8,128)(2,1)} %w_key.1, bf16[2048,256]{1,0:T(8,128)(2,1)} %w_value.1, bf16[256,2048]{1,0:T(8,128)(2,1)} %w_out.1, f32[2,2048]{1,0:T(2,128)} %bitcast.3, s32[1,2048]{1,0:T(1,128)} %bitcast.5, ...), custom_call_target="tpu_custom_call" | custom-call | tf_op jit(solution)/shard_map/pallas_call | solution.py:466
  75.0 2.3 %copy.10 = bf16[2048,256]{1,0:T(8,128)(2,1)} copy(bf16[2048,256]{1,0:T(8,128)(2,1)} %shard_map.82) | data formatting | bytes 2097152
where the time goes:
time: 77.4 us; the launch traced here: 77.2 us
  Pallas kernels  75 us (97%)
  local copies, waits for them, and re-layouts  2.26 us (3%)
    pallas_call x1, Pallas kernels, shards(): call(tokens, w_query, w_key, w_value, w_out, decay_rate.T, level_row_inde...  75 us
    unnamed x1, local copies, waits for them, and re-layouts  2.26 us

commit v1 on v0

v1 whole, which is shorter than its diff:
```python
import functools

import jax
import jax.numpy as jnp
from jax import lax
from jax.experimental import pallas as pl
from jax.experimental.pallas import tpu as pltpu
from jax.sharding import PartitionSpec as P

F32, BF16 = jnp.float32, jnp.bfloat16
MESH = pl.DeviceIdType.MESH
EPSILON = 1e-06
DH = 128
HEADS = 2
CHUNK = 256
CHUNKS = 8
HALF = CHUNKS // 2
LOCAL = 3
PLACES_Z, PLACES_Y = 8, 4
CTX_Z, CTX_Y = 3, 2
CROSS = CTX_Z + CTX_Y
TALL = 2
FIRST_LOCAL, FIRST_CROSS = 3, 6
ROWS = 16
CUM = 11
MSG = DH + 16
NEVER = -1e30


def dot(a, b, dims=((1,), (0,))):
    return lax.dot_general(a, b, (dims, ((), ())), preferred_element_type=F32)


def split(x, terms):
    parts = []
    for _ in range(terms):
        part = x.astype(BF16)
        parts.append(part)
        x = x - part.astype(F32)
    return parts


def kernel(
    tokens, w_query, w_key, w_value, w_out, rates, row_index, table,
    out,
    tok, wkv, wq, kv, local_states, local_out, cross_lhs, cross_states,
    table_rows, table_parts, rate_rows, cum_rows, offset_rows, send_state, recv_state,
    gathered, other, weights, spare, staged,
    tok_sem, w_sem, wl_sem, ws_send, ws_recv, wx_send, wx_recv,
    st_send, st_recv, g_send, g_recv, out_send, out_recv,
):
    pos = lax.axis_index("ctx")
    me = lax.axis_index("head")
    x = lax.div(me, 2)
    core = lax.rem(me, 2)
    pair = x + 1 - 2 * lax.rem(x, 2)
    across = 3 - x
    far = lax.rem(x + 2, 4)
    z = lax.rem(pos, PLACES_Z)
    y = lax.div(pos, PLACES_Z)
    sibling_id = (pos, 2 * x + 1 - core)
    pair_id = (pos, 2 * pair + core)
    across_id = (pos, 2 * across + core)
    far_id = (pos, 2 * far + core)
    z_bits = [lax.rem(lax.div(z, 2**b), 2) for b in range(CTX_Z)]
    flips = [2**b * (1 - 2 * z_bits[b]) for b in range(CTX_Z)]
    state_ids = [(pos + shift, me) for shift in (flips[0], flips[1], flips[1] + flips[2])]
    state_ids += [(lax.rem(y + d, PLACES_Y) * PLACES_Z + z, me) for d in range(1, PLACES_Y)]
    partners = [sibling_id, pair_id, across_id, far_id] + state_ids

    barrier = pltpu.get_barrier_semaphore()
    for partner in partners:
        pl.semaphore_signal(barrier, inc=1, device_id=partner, device_id_type=MESH)

    def weight_copy(source, head, part):
        return pltpu.make_async_copy(
            source.at[:, pl.ds(head * DH, DH)],
            wkv.at[head, :, pl.ds(part * DH, DH)],
            w_sem.at[head * 2 + part],
        )

    def token_rows(u, count):
        return pl.ds(pl.multiple_of(u * CHUNK, CHUNK), count * CHUNK)

    def token_copy(u):
        return pltpu.make_async_copy(
            tokens.at[token_rows(u, 1), :], tok.at[token_rows(u, 1), :], tok_sem.at[u]
        )

    query_copy = pltpu.make_async_copy(w_query, wq, w_sem.at[4])
    weight_copy(w_key, 0, 0).start()
    weight_copy(w_value, 0, 1).start()
    for u in range(CHUNKS):
        token_copy(u).start()
    weight_copy(w_key, 1, 0).start()
    weight_copy(w_value, 1, 1).start()
    query_copy.start()

    homes = [(weights, 0, 0, x), (weights, 0, 1, across), (spare, None, 0, far), (spare, None, 1, pair)]

    def piece(buffer, slot, a, k):
        view = buffer.at[slot, a] if slot is not None else buffer.at[a]
        return view.at[:, k]

    own_pieces, sibling_pieces = [], []
    for i, (buffer, slot, a, chip) in enumerate(homes):
        columns = pl.ds(pl.multiple_of((2 * chip + core) * 256, 256), 256)
        own_pieces.append(
            pltpu.make_async_copy(w_out.at[:, :, columns], piece(buffer, slot, a, 0), wl_sem.at[i])
        )
        columns = pl.ds(pl.multiple_of((2 * chip + 1 - core) * 256, 256), 256)
        sibling_pieces.append(
            pltpu.make_async_remote_copy(
                src_ref=w_out.at[:, :, columns],
                dst_ref=piece(buffer, slot, a, 1),
                send_sem=ws_send.at[i],
                recv_sem=ws_recv.at[i],
                device_id=sibling_id,
                device_id_type=MESH,
            )
        )

    def weight_send(i, source, slot, target):
        return pltpu.make_async_remote_copy(
            src_ref=source, dst_ref=weights.at[slot], send_sem=wx_send.at[i],
            recv_sem=wx_recv.at[i], device_id=target, device_id_type=MESH,
        )

    weight_sends = [
        weight_send(0, weights.at[0], 2, across_id),
        weight_send(1, spare, 1, pair_id),
        weight_send(2, spare, 3, far_id),
    ]

    for u in range(CHUNKS):
        rate_rows[HEADS * u : HEADS * (u + 1), :] = rates[:, u * CHUNK : (u + 1) * CHUNK]
    before = lax.broadcasted_iota(jnp.int32, (CHUNK, CHUNK), 0)
    after = lax.broadcasted_iota(jnp.int32, (CHUNK, CHUNK), 1)
    upper = (before <= after).astype(BF16)
    cum = sum(dot(part, upper) for part in split(-rate_rows[...], 3))
    cum_rows[...] = cum
    last = cum[:, CHUNK - 1 :]
    key_decay = jnp.exp(last - cum).T
    totals = [[last[HEADS * u + h : HEADS * u + h + 1, :] for u in range(CHUNKS)] for h in range(HEADS)]

    table_rows[...] = jnp.zeros_like(table_rows)
    levels = table.shape[0]
    for h in range(HEADS):
        table_rows[h * ROWS : h * ROWS + levels, :] = table[:, h, :]
    for i, part in enumerate(split(table_rows[...], 3)):
        table_parts[i] = part
    level = lax.broadcasted_iota(jnp.int32, (ROWS, 128), 0)
    none = jnp.zeros((1, 1), F32)
    for u in range(CHUNKS):
        for h in range(HEADS):
            offset = jnp.where(level >= FIRST_CROSS, sum(totals[h][:u], none), none)
            ends = [none, totals[h][u - 1] if u % 2 else none, sum(totals[h][4:u], none)]
            for bit in range(LOCAL):
                end = ends[bit] if (u >> bit) & 1 else NEVER
                offset = jnp.where(level == FIRST_LOCAL + bit, end, offset)
            offset_rows[HEADS * u + h] = offset

    def key_value(h, i):
        result = dot(tok[token_rows(i * TALL, TALL), :], wkv[h]).astype(BF16)
        for part in range(TALL):
            kv[h, i * TALL + part] = result[part * CHUNK : (part + 1) * CHUNK]

    def chunk_state(h, u):
        decay = key_decay[:, HEADS * u + h : HEADS * u + h + 1]
        decayed = (kv[h, u, :, :DH].astype(F32) * decay).astype(BF16)
        return dot(decayed, kv[h, u, :, DH:], ((0,), (0,)))

    def merge(first, second):
        return jnp.exp(second[1]) * first[0] + second[0], first[1] + second[1]

    running = [None] * HEADS
    passed = [jnp.zeros((1, 1), F32) for _ in range(HEADS)]

    def state_copy(h, b):
        return pltpu.make_async_remote_copy(
            src_ref=send_state.at[h, min(b, CTX_Z)], dst_ref=recv_state.at[h, b], send_sem=st_send.at[h, b],
            recv_sem=st_recv.at[h, b], device_id=state_ids[b], device_id_type=MESH,
        )

    def send(h, b):
        state, total = running[h]
        send_state[h, b, 0:DH, :] = state.astype(BF16)
        row = lax.broadcasted_iota(jnp.int32, (16, DH), 0)
        tail = jnp.zeros((16, DH), F32)
        for i, part in enumerate(split(total, 3)):
            tail = jnp.where(row == i, part.astype(F32), tail)
        send_state[h, b, DH:MSG, :] = tail.astype(BF16)
        for step in [b] if b < CTX_Z else range(CTX_Z, CTX_Z + PLACES_Y - 1):
            state_copy(h, step).start()

    def arrived(h, b):
        state_copy(h, b).wait_recv()
        tail = recv_state[h, b, DH:MSG, :].astype(F32)
        return recv_state[h, b, 0:DH, :].astype(F32), tail[0:1, 0:1] + tail[1:2, 0:1] + tail[2:3, 0:1]

    def keep_cross(h, b, state):
        cross_states[h, b * DH : (b + 1) * DH, :] = state.astype(BF16)

    def receive_z(h, b):
        there, there_total = arrived(h, b)
        is_upper = z_bits[b] == 1
        state, total = running[h]
        low = jnp.where(is_upper, there, state)
        high = jnp.where(is_upper, state, there)
        high_total = jnp.where(is_upper, total, there_total)
        running[h] = (jnp.exp(high_total) * low + high, total + there_total)
        send(h, b + 1)
        keep_cross(h, b, jnp.where(is_upper, jnp.exp(passed[h]) * there, 0.0))
        passed[h] = passed[h] + jnp.where(is_upper, there_total, 0.0)

    def receive_y(h):
        behind = [arrived(h, CTX_Z + d) for d in range(PLACES_Y - 1)]
        is_odd, is_upper = lax.rem(y, 2) == 1, lax.div(y, 2) == 1
        (one, one_total), (two, two_total), (three, _) = behind
        keep_cross(h, CTX_Z, jnp.where(is_odd, jnp.exp(passed[h]) * one, 0.0))
        first, second = jnp.where(is_odd, three, two), jnp.where(is_odd, two, one)
        second_total = jnp.where(is_odd, two_total, one_total)
        ahead = passed[h] + jnp.where(is_odd, one_total, 0.0)
        both = jnp.exp(ahead) * (jnp.exp(second_total) * first + second)
        keep_cross(h, CTX_Z + 1, jnp.where(is_upper, both, 0.0))

    def own_state(h):
        single = [(chunk_state(h, u), totals[h][u]) for u in range(CHUNKS)]
        pairs = [merge(single[2 * i], single[2 * i + 1]) for i in range(4)]
        quads = [merge(pairs[2 * i], pairs[2 * i + 1]) for i in range(2)]
        running[h] = merge(quads[0], quads[1])
        send(h, 0)
        zero = jnp.zeros((DH, DH), BF16)
        for u in range(CHUNKS):
            lower = [
                single[u - 1][0].astype(BF16) if u & 1 else zero,
                pairs[u // 2 - 1][0].astype(BF16) if u & 2 else zero,
                quads[0][0].astype(BF16) if u & 4 else zero,
            ]
            for i, state in enumerate(lower):
                local_states[h, u, i * DH : (i + 1) * DH, :] = state

    weight_copy(w_key, 0, 0).wait()
    weight_copy(w_value, 0, 1).wait()

    def first_head(i, carry):
        for part in range(TALL):
            token_copy(i * TALL + part).wait()
        key_value(0, i)
        return carry

    def second_head(i, carry):
        key_value(1, i)
        return carry

    for copy in own_pieces:
        copy.start()
    lax.fori_loop(0, 1, first_head, 0)
    pl.semaphore_wait(barrier, len(partners))
    for copy in sibling_pieces:
        copy.start()
    lax.fori_loop(1, 3, first_head, 0)
    for copy in own_pieces:
        copy.wait()
    for copy in sibling_pieces:
        copy.wait_recv()
    for copy in weight_sends:
        copy.start()
    lax.fori_loop(3, CHUNKS // TALL, first_head, 0)
    own_state(0)

    weight_copy(w_key, 1, 0).wait()
    weight_copy(w_value, 1, 1).wait()
    lax.fori_loop(0, CHUNKS // TALL, second_head, 0)
    receive_z(0, 0)
    own_state(1)
    query_copy.wait()

    def local_part(u, carry):
        queries = dot(tok[token_rows(u, 1), :], wq[...]).astype(BF16)
        slots = table.shape[2]
        chosen = lax.broadcasted_iota(jnp.int32, (slots, CHUNK), 0) == row_index[:, token_rows(u, 1)]
        chosen = jnp.where(chosen, 1.0, 0.0).astype(BF16)
        level_mix = sum(dot(table_parts[i], chosen) for i in range(3))
        row = lax.broadcasted_iota(jnp.int32, (ROWS, CHUNK), 0)
        rows = []
        for h in range(HEADS):
            cum_row = cum_rows[pl.ds(HEADS * u + h, 1), :]
            decay = cum_row + offset_rows[HEADS * u + h][:, 0:1]
            factor = jnp.exp(jnp.where(row >= FIRST_LOCAL, decay, 0.0))
            scaled = level_mix[h * ROWS : (h + 1) * ROWS, :] * factor
            rows.append(jnp.where(row == CUM, cum_row, scaled))
        cols = jnp.concatenate(rows, axis=0).T
        token = lax.broadcasted_iota(jnp.int32, (CHUNK, CHUNK), 0)
        source = lax.broadcasted_iota(jnp.int32, (CHUNK, CHUNK), 1)
        causal = token >= source
        same_block = lax.div(token, 64) == lax.div(source, 64)
        same_pair = lax.div(token, 128) == lax.div(source, 128)
        for h in range(HEADS):
            column = lambda row: cols[:, h * ROWS + row : h * ROWS + row + 1]
            query = queries[:, h * DH : (h + 1) * DH]
            key, value = kv[h, u, :, 0:DH], kv[h, u, :, DH : 2 * DH]
            gap = column(CUM) - cum_rows[pl.ds(HEADS * u + h, 1), :]
            decay = jnp.exp(jnp.where(causal, gap, NEVER))
            mix = jnp.where(same_block, column(0), jnp.where(same_pair, column(1), column(2)))
            scores = dot(query, key, ((1,), (1,)))
            result = dot((scores * decay * mix).astype(BF16), value)
            query = query.astype(F32)
            lhs = [(query * column(FIRST_LOCAL + i)).astype(BF16) for i in range(LOCAL)]
            result += dot(jnp.concatenate(lhs, axis=1), local_states[h, u])
            local_out[u, :, h * DH : (h + 1) * DH] = result
            for i in range(CROSS):
                cross_lhs[u, h, :, i * DH : (i + 1) * DH] = (
                    query * column(FIRST_CROSS + i)
                ).astype(BF16)
        return carry

    lax.fori_loop(0, 2, local_part, 0)
    receive_z(1, 0)
    receive_z(0, 1)
    lax.fori_loop(2, 5, local_part, 0)
    receive_z(1, 1)
    receive_z(0, 2)
    lax.fori_loop(5, CHUNKS, local_part, 0)
    receive_z(1, 2)

    mine = lax.div(x, 2)

    def slot(j, h, number):
        return gathered.at[j, h, :, pl.ds(number * DH, DH)]

    def moved(kind, source, target_slot, target):
        def copy(j, h):
            from_ref = other.at[j, h] if source is None else slot(j, h, source)
            return pltpu.make_async_remote_copy(
                src_ref=from_ref, dst_ref=slot(j, h, target_slot), send_sem=g_send.at[kind, j, h],
                recv_sem=g_recv.at[kind, j, h], device_id=target, device_id_type=MESH,
            )

        return copy

    own_to_sibling = moved(0, 0, 1, sibling_id)
    own_to_pair = moved(1, 0, 2, pair_id)
    pair_to_sibling = moved(2, 2, 3, sibling_id)
    other_to_across = moved(3, None, 4, across_id)
    across_to_sibling = moved(4, 4, 5, sibling_id)
    across_to_pair = moved(5, 4, 6, pair_id)
    far_to_sibling = moved(6, 6, 7, sibling_id)
    moves = (
        own_to_sibling, own_to_pair, pair_to_sibling, other_to_across,
        across_to_sibling, across_to_pair, far_to_sibling,
    )

    def mine_rows(j):
        return pl.ds(pl.multiple_of((mine * HALF + j) * CHUNK, CHUNK), CHUNK)

    def result_to_across(j):
        return pltpu.make_async_remote_copy(
            src_ref=staged.at[j], dst_ref=out.at[mine_rows(j), :], send_sem=out_send.at[j],
            recv_sem=out_recv.at[j], device_id=across_id, device_id_type=MESH,
        )

    def normed(u, h):
        value = local_out[u, :, h * DH : (h + 1) * DH] + dot(cross_lhs[u, h], cross_states[h])
        square = jnp.mean(value * value, axis=1, keepdims=True)
        return (value * lax.rsqrt(square + EPSILON)).astype(BF16)

    def finish(h):
        def step(j, carry):
            other[j, h] = normed((1 - mine) * HALF + j, h)
            other_to_across(j, h).start()
            gathered[j, h, :, 0:DH] = normed(mine * HALF + j, h)
            if h == 0:
                own_to_pair(j, h).start()
            own_to_sibling(j, h).start()
            return carry

        lax.fori_loop(0, HALF, step, 0)

    receive_y(0)
    finish(0)
    receive_y(1)
    finish(1)

    def forward(j, carry):
        own_to_pair(j, 1).start()
        for h in range(HEADS):
            other_to_across(j, h).wait_recv()
            across_to_pair(j, h).start()
            across_to_sibling(j, h).start()
        return carry

    lax.fori_loop(0, HALF, forward, 0)
    for copy in weight_sends:
        copy.wait_recv()

    for_own, for_across = (0, 1, 1, 0), (1, 0, 0, 1)

    def project(j, carry):
        def product(a, r):
            return sum(
                dot(gathered[j, h, :, r * 256 : (r + 1) * 256], weights[r, a[r], h].reshape(256, 256))
                for h in range(HEADS)
            )

        for h in range(HEADS):
            own_to_sibling(j, h).wait_recv()
            across_to_sibling(j, h).wait_recv()
            own_to_pair(j, h).wait_recv()
            pair_to_sibling(j, h).start()
        to_across = product(for_across, 0) + product(for_across, 2)
        to_own = product(for_own, 0) + product(for_own, 2)
        for h in range(HEADS):
            across_to_pair(j, h).wait_recv()
            far_to_sibling(j, h).start()
        for h in range(HEADS):
            pair_to_sibling(j, h).wait_recv()
        to_across += product(for_across, 1)
        to_own += product(for_own, 1)
        for h in range(HEADS):
            far_to_sibling(j, h).wait_recv()
        staged[j] = (to_across + product(for_across, 3)).astype(BF16)
        result_to_across(j).start()
        out[mine_rows(j), :] = (to_own + product(for_own, 3)).astype(BF16)
        return carry

    lax.fori_loop(0, HALF, project, 0)

    def drain(j, carry):
        for copy in moves:
            for h in range(HEADS):
                copy(j, h).wait_send()
        result_to_across(j).wait()
        return carry

    lax.fori_loop(0, HALF, drain, 0)
    for copy in sibling_pieces + weight_sends:
        copy.wait_send()
    for h in range(HEADS):
        for b in range(CTX_Z + PLACES_Y - 1):
            state_copy(h, b).wait_send()


def shards(tokens, w_query, w_key, w_value, w_out, decay_rate, level_row_index, level_weight_table):
    rows, depth = tokens.shape
    width = w_query.shape[1]
    vmem = functools.partial(pltpu.VMEM)
    dma = pltpu.SemaphoreType.DMA
    hbm, on_chip = pl.BlockSpec(memory_space=pl.ANY), pl.BlockSpec(memory_space=pltpu.VMEM)
    call = pl.pallas_call(
        kernel,
        out_shape=pltpu.VMEM((rows, width), BF16),
        in_specs=[hbm] * 5 + [on_chip] * 3,
        out_specs=on_chip,
        scratch_shapes=[
            vmem((rows, depth), BF16),
            vmem((HEADS, depth, 2 * DH), BF16),
            vmem((depth, width), BF16),
            vmem((HEADS, CHUNKS, CHUNK, 2 * DH), BF16),
            vmem((HEADS, CHUNKS, LOCAL * DH, DH), BF16),
            vmem((CHUNKS, CHUNK, width), F32),
            vmem((CHUNKS, HEADS, CHUNK, CROSS * DH), BF16),
            vmem((HEADS, CROSS * DH, DH), BF16),
            vmem((HEADS * ROWS, level_weight_table.shape[0]), F32),
            vmem((3, HEADS * ROWS, level_weight_table.shape[0]), BF16),
            vmem((HEADS * CHUNKS, CHUNK), F32),
            vmem((HEADS * CHUNKS, CHUNK), F32),
            vmem((HEADS * CHUNKS, ROWS, 128), F32),
            vmem((HEADS, CTX_Z + 1, MSG, DH), BF16),
            vmem((HEADS, CTX_Z + PLACES_Y - 1, MSG, DH), BF16),
            vmem((HALF, HEADS, CHUNK, 8 * DH), BF16),
            vmem((HALF, HEADS, CHUNK, DH), BF16),
            vmem((4, 2, HEADS, 2, DH, width), BF16),
            vmem((2, HEADS, 2, DH, width), BF16),
            vmem((HALF, CHUNK, width), BF16),
            dma((CHUNKS,)), dma((5,)), dma((4,)), dma((4,)), dma((4,)), dma((3,)), dma((3,)),
            dma((HEADS, CTX_Z + PLACES_Y - 1)), dma((HEADS, CTX_Z + PLACES_Y - 1)),
            dma((7, HALF, HEADS)), dma((7, HALF, HEADS)), dma((HALF,)), dma((HALF,)),
        ],
        compiler_params=pltpu.CompilerParams(
            collective_id=0, has_side_effects=True, vmem_limit_bytes=56 * 2**20
        ),
    )
    return call(
        tokens, w_query, w_key, w_value, w_out.reshape(HEADS, DH, -1), decay_rate.T, level_row_index.reshape(1, rows),
        level_weight_table.transpose(2, 1, 0),
    )


def solution(mesh):
    placed = (
        P("ctx", None),
        P(None, "head"),
        P(None, "head"),
        P(None, "head"),
        P("head", None),
        P("ctx", "head"),
        P("ctx"),
        P(None, "head", None),
    )
    return jax.shard_map(
        shards, mesh=mesh, in_specs=placed, out_specs=P("ctx", "head"), check_vma=False
    )
```

time: 77.4 us -> 67 us (0.87)
  Pallas kernels: 75 us -> 65.9 us
  local copies, waits for them, and re-layouts: 2.26 us -> 0.97 us
    pallas_call x1, Pallas kernels: 75 us -> 65.9 us  [shards(): call(tokens, w_query, w_key, w_value, w_out.reshape(HEADS, DH, -1), decay...]
    unnamed x1, local copies, waits for them, and re-layouts: 2.26 us -> 0.97 us
where the time goes in v1:
time: 67 us; the launch traced here: 66.9 us
  Pallas kernels  65.9 us (98%)
  local copies, waits for them, and re-layouts  0.97 us (1%)
    pallas_call x1, Pallas kernels, shards(): call(tokens, w_query, w_key, w_value, w_out.reshape(HEADS, DH, -1), decay...  65.9 us

profile of v1, /device:TPU:1, one launch (start us, length us, event | category | flops | bytes accessed | tf_op | source)
XLA Modules:
  0.0 66.9 jit_solution(6787845409838443443)
XLA Ops:
  0.0 65.9 %shard_map.82 = bf16[2048,256]{1,0:T(8,128)(2,1)S(1)} custom-call(bf16[2048,2048]{1,0:T(8,128)(2,1)} %tokens.1, bf16[2048,256]{1,0:T(8,128)(2,1)} %w_query.1, bf16[2048,256]{1,0:T(8,128)(2,1)} %w_key.1, bf16[2048,256]{1,0:T(8,128)(2,1)} %w_value.1, bf16[2,128,2048]{2,1,0:T(8,128)(2,1)} %bitcast.4, f32[2,2048]{1,0:T(2,128)} %bitcast.5, s32[1,2048]{1,0:T(1,128)} %bitcast.7, ...), custom_call_target="tpu_custom_call" | custom-call | tf_op jit(solution)/shard_map/pallas_call | solution.py:484
  65.9 1.0 %copy.10 = bf16[2048,256]{1,0:T(8,128)(2,1)} copy(bf16[2048,256]{1,0:T(8,128)(2,1)S(1)} %shard_map.82) | data formatting | bytes 2097152

commit v2 on v1

--- a/solution.py
+++ b/solution.py
@@ -15,6 +15,9 @@
 CHUNK = 256
 CHUNKS = 8
 HALF = CHUNKS // 2
+PIECE = 128
+PIECES = HALF * CHUNK // PIECE
+LAG = 4
 LOCAL = 3
 PLACES_Z, PLACES_Y = 8, 4
 CTX_Z, CTX_Y = 3, 2
@@ -45,9 +48,9 @@
     out,
     tok, wkv, wq, kv, local_states, local_out, cross_lhs, cross_states,
     table_rows, table_parts, rate_rows, cum_rows, offset_rows, send_state, recv_state,
-    gathered, other, weights, spare, staged,
-    tok_sem, w_sem, wl_sem, ws_send, ws_recv, wx_send, wx_recv,
-    st_send, st_recv, g_send, g_recv, out_send, out_recv,
+    gathered, other, weights, spare, partial, their_partial, own_partial, staged,
+    tok_sem, w_sem, wl_sem, wx_send, wx_recv,
+    st_send, st_recv, g_send, g_recv, p_send, p_recv, out_send, out_recv,
 ):
     pos = lax.axis_index("ctx")
     me = lax.axis_index("head")
@@ -92,44 +95,30 @@
     weight_copy(w_value, 0, 1).start()
     for u in range(CHUNKS):
         token_copy(u).start()
-    weight_copy(w_key, 1, 0).start()
-    weight_copy(w_value, 1, 1).start()
-    query_copy.start()
-
-    homes = [(weights, 0, 0, x), (weights, 0, 1, across), (spare, None, 0, far), (spare, None, 1, pair)]
-
-    def piece(buffer, slot, a, k):
-        view = buffer.at[slot, a] if slot is not None else buffer.at[a]
-        return view.at[:, k]
-
-    own_pieces, sibling_pieces = [], []
-    for i, (buffer, slot, a, chip) in enumerate(homes):
-        columns = pl.ds(pl.multiple_of((2 * chip + core) * 256, 256), 256)
-        own_pieces.append(
-            pltpu.make_async_copy(w_out.at[:, :, columns], piece(buffer, slot, a, 0), wl_sem.at[i])
-        )
-        columns = pl.ds(pl.multiple_of((2 * chip + 1 - core) * 256, 256), 256)
-        sibling_pieces.append(
-            pltpu.make_async_remote_copy(
-                src_ref=w_out.at[:, :, columns],
-                dst_ref=piece(buffer, slot, a, 1),
-                send_sem=ws_send.at[i],
-                recv_sem=ws_recv.at[i],
-                device_id=sibling_id,
-                device_id_type=MESH,
+
+    homes = [(weights.at[0], 0, x), (weights.at[0], 1, across), (spare, 0, far), (spare, 1, pair)]
+    own_pieces = []
+    for i, (buffer, a, chip) in enumerate(homes):
+        for k, side in enumerate((core, 1 - core)):
+            columns = pl.ds(pl.multiple_of((2 * chip + side) * 256, 256), 256)
+            own_pieces.append(
+                pltpu.make_async_copy(w_out.at[:, columns], buffer.at[2 * a + k], wl_sem.at[2 * i + k])
             )
-        )
-
-    def weight_send(i, source, slot, target):
+
+    def weight_send(i, source, target_ref, target):
         return pltpu.make_async_remote_copy(
-            src_ref=source, dst_ref=weights.at[slot], send_sem=wx_send.at[i],
+            src_ref=source, dst_ref=target_ref, send_sem=wx_send.at[i],
             recv_sem=wx_recv.at[i], device_id=target, device_id_type=MESH,
         )
 
     weight_sends = [
-        weight_send(0, weights.at[0], 2, across_id),
-        weight_send(1, spare, 1, pair_id),
-        weight_send(2, spare, 3, far_id),
+        weight_send(0, spare.at[y], weights.at[3, y], far_id),
+        weight_send(1, weights.at[0], weights.at[2], across_id),
+        weight_send(2, spare, weights.at[1], pair_id),
+    ]
+    far_sends = [
+        weight_send(2 + d, weights.at[3, y], weights.at[3, y], state_ids[CTX_Z + d - 1])
+        for d in range(1, PLACES_Y)
     ]
 
     for u in range(CHUNKS):
@@ -255,15 +244,14 @@
 
     for copy in own_pieces:
         copy.start()
+    weight_copy(w_key, 1, 0).start()
+    weight_copy(w_value, 1, 1).start()
+    query_copy.start()
     lax.fori_loop(0, 1, first_head, 0)
     pl.semaphore_wait(barrier, len(partners))
-    for copy in sibling_pieces:
-        copy.start()
     lax.fori_loop(1, 3, first_head, 0)
     for copy in own_pieces:
         copy.wait()
-    for copy in sibling_pieces:
-        copy.wait_recv()
     for copy in weight_sends:
         copy.start()
     lax.fori_loop(3, CHUNKS // TALL, first_head, 0)
@@ -275,6 +263,9 @@
     receive_z(0, 0)
     own_state(1)
     query_copy.wait()
+    weight_sends[0].wait_recv()
+    for copy in far_sends:
+        copy.start()
 
     def local_part(u, carry):
         queries = dot(tok[token_rows(u, 1), :], wq[...]).astype(BF16)
@@ -291,6 +282,7 @@
             scaled = level_mix[h * ROWS : (h + 1) * ROWS, :] * factor
             rows.append(jnp.where(row == CUM, cum_row, scaled))
         cols = jnp.concatenate(rows, axis=0).T
+        cols16 = cols.astype(BF16)
         token = lax.broadcasted_iota(jnp.int32, (CHUNK, CHUNK), 0)
         source = lax.broadcasted_iota(jnp.int32, (CHUNK, CHUNK), 1)
         causal = token >= source
@@ -305,54 +297,46 @@
             mix = jnp.where(same_block, column(0), jnp.where(same_pair, column(1), column(2)))
             scores = dot(query, key, ((1,), (1,)))
             result = dot((scores * decay * mix).astype(BF16), value)
-            query = query.astype(F32)
-            lhs = [(query * column(FIRST_LOCAL + i)).astype(BF16) for i in range(LOCAL)]
+            column16 = lambda row: cols16[:, h * ROWS + row : h * ROWS + row + 1]
+            lhs = [query * column16(FIRST_LOCAL + i) for i in range(LOCAL)]
             result += dot(jnp.concatenate(lhs, axis=1), local_states[h, u])
             local_out[u, :, h * DH : (h + 1) * DH] = result
             for i in range(CROSS):
-                cross_lhs[u, h, :, i * DH : (i + 1) * DH] = (
-                    query * column(FIRST_CROSS + i)
-                ).astype(BF16)
+                cross_lhs[u, h, :, i * DH : (i + 1) * DH] = query * column16(FIRST_CROSS + i)
         return carry
 
     lax.fori_loop(0, 2, local_part, 0)
+    receive_z(0, 1)
     receive_z(1, 0)
-    receive_z(0, 1)
     lax.fori_loop(2, 5, local_part, 0)
+    receive_z(0, 2)
     receive_z(1, 1)
-    receive_z(0, 2)
     lax.fori_loop(5, CHUNKS, local_part, 0)
-    receive_z(1, 2)
 
     mine = lax.div(x, 2)
-
-    def slot(j, h, number):
-        return gathered.at[j, h, :, pl.ds(number * DH, DH)]
 
     def moved(kind, source, target_slot, target):
         def copy(j, h):
-            from_ref = other.at[j, h] if source is None else slot(j, h, source)
             return pltpu.make_async_remote_copy(
-                src_ref=from_ref, dst_ref=slot(j, h, target_slot), send_sem=g_send.at[kind, j, h],
+                src_ref=other.at[j, h] if source is None else gathered.at[j, h, source],
+                dst_ref=gathered.at[j, h, target_slot], send_sem=g_send.at[kind, j, h],
                 recv_sem=g_recv.at[kind, j, h], device_id=target, device_id_type=MESH,
             )
 
         return copy
 
-    own_to_sibling = moved(0, 0, 1, sibling_id)
-    own_to_pair = moved(1, 0, 2, pair_id)
-    pair_to_sibling = moved(2, 2, 3, sibling_id)
-    other_to_across = moved(3, None, 4, across_id)
-    across_to_sibling = moved(4, 4, 5, sibling_id)
-    across_to_pair = moved(5, 4, 6, pair_id)
-    far_to_sibling = moved(6, 6, 7, sibling_id)
-    moves = (
-        own_to_sibling, own_to_pair, pair_to_sibling, other_to_across,
-        across_to_sibling, across_to_pair, far_to_sibling,
-    )
+    own_to_pair = moved(0, 0, 1, pair_id)
+    other_to_across = moved(1, None, 2, across_id)
+    across_to_pair = moved(2, 2, 3, pair_id)
+
+    def partial_to_sibling(j):
+        return pltpu.make_async_remote_copy(
+            src_ref=partial.at[j], dst_ref=their_partial.at[j], send_sem=p_send.at[j],
+            recv_sem=p_recv.at[j], device_id=sibling_id, device_id_type=MESH,
+        )
 
     def mine_rows(j):
-        return pl.ds(pl.multiple_of((mine * HALF + j) * CHUNK, CHUNK), CHUNK)
+        return pl.ds(pl.multiple_of((mine * PIECES + j) * PIECE, PIECE), PIECE)
 
     def result_to_across(j):
         return pltpu.make_async_remote_copy(
@@ -367,74 +351,91 @@
 
     def finish(h):
         def step(j, carry):
-            other[j, h] = normed((1 - mine) * HALF + j, h)
-            other_to_across(j, h).start()
-            gathered[j, h, :, 0:DH] = normed(mine * HALF + j, h)
-            if h == 0:
-                own_to_pair(j, h).start()
-            own_to_sibling(j, h).start()
+            theirs = normed((1 - mine) * HALF + j, h)
+            for part in range(CHUNK // PIECE):
+                here = j * (CHUNK // PIECE) + part
+                other[here, h] = theirs[part * PIECE : (part + 1) * PIECE]
+                other_to_across(here, h).start()
+            ours = normed(mine * HALF + j, h)
+            for part in range(CHUNK // PIECE):
+                here = j * (CHUNK // PIECE) + part
+                gathered[here, h, 0] = ours[part * PIECE : (part + 1) * PIECE]
+                if h == 0:
+                    own_to_pair(here, h).start()
             return carry
 
         lax.fori_loop(0, HALF, step, 0)
 
     receive_y(0)
+    receive_z(1, 2)
     finish(0)
     receive_y(1)
     finish(1)
 
-    def forward(j, carry):
+    for_own, for_across = (0, 1, 1, 0), (1, 0, 0, 1)
+
+    def forward(j):
         own_to_pair(j, 1).start()
         for h in range(HEADS):
             other_to_across(j, h).wait_recv()
             across_to_pair(j, h).start()
-            across_to_sibling(j, h).start()
+
+    def project(j):
+        def product(r, a, k):
+            both = jnp.concatenate([gathered[j, h, r] for h in range(HEADS)], axis=1)
+            return dot(both, weights[r, 2 * a[r] + k])
+
+        for h in range(HEADS):
+            own_to_pair(j, h).wait_recv()
+            across_to_pair(j, h).wait_recv()
+        for k in (1, 0):
+            for i, a in enumerate((for_across, for_own)):
+                result = sum(product(r, a, k) for r in range(4))
+                if k == 1:
+                    partial[j, i] = result.astype(BF16)
+                else:
+                    own_partial[j, i] = result
+            if k == 1:
+                partial_to_sibling(j).start()
+
+    def deliver(j):
+        partial_to_sibling(j).wait_recv()
+        staged[j] = (own_partial[j, 0] + their_partial[j, 0].astype(F32)).astype(BF16)
+        result_to_across(j).start()
+        out[mine_rows(j), :] = (own_partial[j, 1] + their_partial[j, 1].astype(F32)).astype(BF16)
+
+    def step(j, carry):
+        @pl.when(j < PIECES)
+        def _():
+            forward(j)
+
+        @pl.when(j == LAG)
+        def _():
+            for copy in weight_sends[1:] + far_sends:
+                copy.wait_recv()
+
+        @pl.when((j >= LAG) & (j < PIECES + LAG))
+        def _():
+            project(j - LAG)
+
+        @pl.when(j > LAG)
+        def _():
+            deliver(j - LAG - 1)
+
         return carry
 
-    lax.fori_loop(0, HALF, forward, 0)
-    for copy in weight_sends:
-        copy.wait_recv()
-
-    for_own, for_across = (0, 1, 1, 0), (1, 0, 0, 1)
-
-    def project(j, carry):
-        def product(a, r):
-            return sum(
-                dot(gathered[j, h, :, r * 256 : (r + 1) * 256], weights[r, a[r], h].reshape(256, 256))
-                for h in range(HEADS)
-            )
-
-        for h in range(HEADS):
-            own_to_sibling(j, h).wait_recv()
-            across_to_sibling(j, h).wait_recv()
-            own_to_pair(j, h).wait_recv()
-            pair_to_sibling(j, h).start()
-        to_across = product(for_across, 0) + product(for_across, 2)
-        to_own = product(for_own, 0) + product(for_own, 2)
-        for h in range(HEADS):
-            across_to_pair(j, h).wait_recv()
-            far_to_sibling(j, h).start()
-        for h in range(HEADS):
-            pair_to_sibling(j, h).wait_recv()
-        to_across += product(for_across, 1)
-        to_own += product(for_own, 1)
-        for h in range(HEADS):
-            far_to_sibling(j, h).wait_recv()
-        staged[j] = (to_across + product(for_across, 3)).astype(BF16)
-        result_to_across(j).start()
-        out[mine_rows(j), :] = (to_own + product(for_own, 3)).astype(BF16)
-        return carry
-
-    lax.fori_loop(0, HALF, project, 0)
+    lax.fori_loop(0, PIECES + LAG + 1, step, 0)
 
     def drain(j, carry):
-        for copy in moves:
+        for copy in (own_to_pair, other_to_across, across_to_pair):
             for h in range(HEADS):
                 copy(j, h).wait_send()
+        partial_to_sibling(j).wait_send()
         result_to_across(j).wait()
         return carry
 
-    lax.fori_loop(0, HALF, drain, 0)
-    for copy in sibling_pieces + weight_sends:
+    lax.fori_loop(0, PIECES, drain, 0)
+    for copy in weight_sends + far_sends:
         copy.wait_send()
     for h in range(HEADS):
         for b in range(CTX_Z + PLACES_Y - 1):
@@ -468,21 +469,26 @@
             vmem((HEADS * CHUNKS, ROWS, 128), F32),
             vmem((HEADS, CTX_Z + 1, MSG, DH), BF16),
             vmem((HEADS, CTX_Z + PLACES_Y - 1, MSG, DH), BF16),
-            vmem((HALF, HEADS, CHUNK, 8 * DH), BF16),
-            vmem((HALF, HEADS, CHUNK, DH), BF16),
-            vmem((4, 2, HEADS, 2, DH, width), BF16),
-            vmem((2, HEADS, 2, DH, width), BF16),
-            vmem((HALF, CHUNK, width), BF16),
-            dma((CHUNKS,)), dma((5,)), dma((4,)), dma((4,)), dma((4,)), dma((3,)), dma((3,)),
+            vmem((PIECES, HEADS, 4, PIECE, DH), BF16),
+            vmem((PIECES, HEADS, PIECE, DH), BF16),
+            vmem((4, 4, width, width), BF16),
+            vmem((4, width, width), BF16),
+            vmem((PIECES, 2, PIECE, width), BF16),
+            vmem((PIECES, 2, PIECE, width), BF16),
+            vmem((PIECES, 2, PIECE, width), F32),
+            vmem((PIECES, PIECE, width), BF16),
+            dma((CHUNKS,)), dma((5,)), dma((8,)), dma((6,)), dma((6,)),
             dma((HEADS, CTX_Z + PLACES_Y - 1)), dma((HEADS, CTX_Z + PLACES_Y - 1)),
-            dma((7, HALF, HEADS)), dma((7, HALF, HEADS)), dma((HALF,)), dma((HALF,)),
+
+            dma((3, PIECES, HEADS)), dma((3, PIECES, HEADS)),
+            dma((PIECES,)), dma((PIECES,)), dma((PIECES,)), dma((PIECES,)),
         ],
         compiler_params=pltpu.CompilerParams(
             collective_id=0, has_side_effects=True, vmem_limit_bytes=56 * 2**20
         ),
     )
     return call(
-        tokens, w_query, w_key, w_value, w_out.reshape(HEADS, DH, -1), decay_rate.T, level_row_index.reshape(1, rows),
+        tokens, w_query, w_key, w_value, w_out, decay_rate.T, level_row_index.reshape(1, rows),
         level_weight_table.transpose(2, 1, 0),
     )
 

time: 67 us -> 63.6 us (0.949)
  Pallas kernels: 65.9 us -> 62.5 us
    pallas_call x1, Pallas kernels: 65.9 us -> 62.5 us  [shards(): call(tokens, w_query, w_key, w_value, w_out, decay_rate.T, level_row_inde...]
where the time goes in v2:
time: 63.6 us; the launch traced here: 63.4 us
  Pallas kernels  62.5 us (98%)
  local copies, waits for them, and re-layouts  0.97 us (2%)
    pallas_call x1, Pallas kernels, shards(): call(tokens, w_query, w_key, w_value, w_out, decay_rate.T, level_row_inde...  62.5 us

profile of v2, /device:TPU:1, one launch (start us, length us, event | category | flops | bytes accessed | tf_op | source)
XLA Modules:
  0.0 63.4 jit_solution(5008753943187604282)
XLA Ops:
  0.0 62.5 %shard_map.82 = bf16[2048,256]{1,0:T(8,128)(2,1)S(1)} custom-call(bf16[2048,2048]{1,0:T(8,128)(2,1)} %tokens.1, bf16[2048,256]{1,0:T(8,128)(2,1)} %w_query.1, bf16[2048,256]{1,0:T(8,128)(2,1)} %w_key.1, bf16[2048,256]{1,0:T(8,128)(2,1)} %w_value.1, bf16[256,2048]{1,0:T(8,128)(2,1)} %w_out.1, f32[2,2048]{1,0:T(2,128)} %bitcast.3, s32[1,2048]{1,0:T(1,128)} %bitcast.5, ...), custom_call_target="tpu_custom_call" | custom-call | tf_op jit(solution)/shard_map/pallas_call | solution.py:490
  62.5 1.0 %copy.10 = bf16[2048,256]{1,0:T(8,128)(2,1)} copy(bf16[2048,256]{1,0:T(8,128)(2,1)S(1)} %shard_map.82) | data formatting | bytes 2097152

commit v3 on v2

--- a/solution.py
+++ b/solution.py
@@ -17,7 +17,8 @@
 HALF = CHUNKS // 2
 PIECE = 128
 PIECES = HALF * CHUNK // PIECE
-LAG = 4
+LAST, EXTRA = PIECES - 1, PIECES
+LAG = 3
 LOCAL = 3
 PLACES_Z, PLACES_Y = 8, 4
 CTX_Z, CTX_Y = 3, 2
@@ -44,13 +45,14 @@
 
 
 def kernel(
-    tokens, w_query, w_key, w_value, w_out, rates, row_index, table,
+    tokens, w_query, w_key, w_value, w_out, rates_in, row_index_in, table_in,
     out,
+    rates, row_index, table, small_sem,
     tok, wkv, wq, kv, local_states, local_out, cross_lhs, cross_states,
     table_rows, table_parts, rate_rows, cum_rows, offset_rows, send_state, recv_state,
     gathered, other, weights, spare, partial, their_partial, own_partial, staged,
     tok_sem, w_sem, wl_sem, wx_send, wx_recv,
-    st_send, st_recv, g_send, g_recv, p_send, p_recv, out_send, out_recv,
+    st_send, st_recv, g_send, g_recv, x_send, x_recv, p_send, p_recv, out_send, out_recv,
 ):
     pos = lax.axis_index("ctx")
     me = lax.axis_index("head")
@@ -90,6 +92,12 @@
             tokens.at[token_rows(u, 1), :], tok.at[token_rows(u, 1), :], tok_sem.at[u]
         )
 
+    small = [
+        pltpu.make_async_copy(source, target, small_sem.at[i])
+        for i, (source, target) in enumerate(((rates_in, rates), (row_index_in, row_index), (table_in, table)))
+    ]
+    for copy in small:
+        copy.start()
     query_copy = pltpu.make_async_copy(w_query, wq, w_sem.at[4])
     weight_copy(w_key, 0, 0).start()
     weight_copy(w_value, 0, 1).start()
@@ -120,6 +128,9 @@
         weight_send(2 + d, weights.at[3, y], weights.at[3, y], state_ids[CTX_Z + d - 1])
         for d in range(1, PLACES_Y)
     ]
+
+    for copy in small:
+        copy.wait()
 
     for u in range(CHUNKS):
         rate_rows[HEADS * u : HEADS * (u + 1), :] = rates[:, u * CHUNK : (u + 1) * CHUNK]
@@ -329,6 +340,21 @@
     other_to_across = moved(1, None, 2, across_id)
     across_to_pair = moved(2, 2, 3, pair_id)
 
+    def moved_extra(kind, piece, source, target_slot, target):
+        def copy(h):
+            return pltpu.make_async_remote_copy(
+                src_ref=gathered.at[piece, h, source], dst_ref=gathered.at[EXTRA, h, target_slot],
+                send_sem=x_send.at[kind, h], recv_sem=x_recv.at[kind, h],
+                device_id=target, device_id_type=MESH,
+            )
+
+        return copy
+
+    extra_to_pair = moved_extra(0, EXTRA, 0, 1, pair_id)
+    last_to_across = moved_extra(1, LAST, 0, 2, across_id)
+    last_pair_to_across = moved_extra(2, LAST, 1, 3, across_id)
+    extra_moves = (extra_to_pair, last_to_across, last_pair_to_across)
+
     def partial_to_sibling(j):
         return pltpu.make_async_remote_copy(
             src_ref=partial.at[j], dst_ref=their_partial.at[j], send_sem=p_send.at[j],
@@ -365,6 +391,10 @@
             return carry
 
         lax.fori_loop(0, HALF, step, 0)
+        gathered[EXTRA, h, 0] = other[LAST, h]
+        last_to_across(h).start()
+        if h == 1:
+            own_to_pair(LAST, h).start()
 
     receive_y(0)
     receive_z(1, 2)
@@ -375,28 +405,37 @@
     for_own, for_across = (0, 1, 1, 0), (1, 0, 0, 1)
 
     def forward(j):
-        own_to_pair(j, 1).start()
+        @pl.when(j < LAST)
+        def _():
+            own_to_pair(j, 1).start()
+
         for h in range(HEADS):
             other_to_across(j, h).wait_recv()
             across_to_pair(j, h).start()
 
-    def project(j):
-        def product(r, a, k):
+        @pl.when(j == LAST)
+        def _():
+            for h in range(HEADS):
+                extra_to_pair(h).start()
+                own_to_pair(LAST, h).wait_recv()
+                last_pair_to_across(h).start()
+
+    def product(j, a, k):
+        def term(r):
             both = jnp.concatenate([gathered[j, h, r] for h in range(HEADS)], axis=1)
             return dot(both, weights[r, 2 * a[r] + k])
 
+        return sum(term(r) for r in range(4))
+
+    def project(j):
         for h in range(HEADS):
             own_to_pair(j, h).wait_recv()
             across_to_pair(j, h).wait_recv()
-        for k in (1, 0):
-            for i, a in enumerate((for_across, for_own)):
-                result = sum(product(r, a, k) for r in range(4))
-                if k == 1:
-                    partial[j, i] = result.astype(BF16)
-                else:
-                    own_partial[j, i] = result
-            if k == 1:
-                partial_to_sibling(j).start()
+        for i, a in enumerate((for_across, for_own)):
+            partial[j, i] = product(j, a, 1).astype(BF16)
+        partial_to_sibling(j).start()
+        for i, a in enumerate((for_across, for_own)):
+            own_partial[j, i] = product(j, a, 0)
 
     def deliver(j):
         partial_to_sibling(j).wait_recv()
@@ -414,7 +453,7 @@
             for copy in weight_sends[1:] + far_sends:
                 copy.wait_recv()
 
-        @pl.when((j >= LAG) & (j < PIECES + LAG))
+        @pl.when((j >= LAG) & (j < LAST + LAG))
         def _():
             project(j - LAG)
 
@@ -424,17 +463,38 @@
 
         return carry
 
-    lax.fori_loop(0, PIECES + LAG + 1, step, 0)
+    lax.fori_loop(0, LAST + LAG + 1, step, 0)
+
+    for h in range(HEADS):
+        last_to_across(h).wait_recv()
+        last_pair_to_across(h).wait_recv()
+        across_to_pair(LAST, h).wait_recv()
+        extra_to_pair(h).wait_recv()
+    for i, piece in enumerate((EXTRA, LAST)):
+        partial[LAST, i] = product(piece, for_own, 1).astype(BF16)
+    partial_to_sibling(LAST).start()
+    results = [product(piece, for_own, 0) for piece in (EXTRA, LAST)]
+    partial_to_sibling(LAST).wait_recv()
+    extra_rows = pl.ds(pl.multiple_of(((1 - mine) * PIECES + LAST) * PIECE, PIECE), PIECE)
+    out[extra_rows, :] = (results[0] + their_partial[LAST, 0].astype(F32)).astype(BF16)
+    out[mine_rows(LAST), :] = (results[1] + their_partial[LAST, 1].astype(F32)).astype(BF16)
 
     def drain(j, carry):
         for copy in (own_to_pair, other_to_across, across_to_pair):
             for h in range(HEADS):
                 copy(j, h).wait_send()
         partial_to_sibling(j).wait_send()
+        return carry
+
+    def drain_results(j, carry):
         result_to_across(j).wait()
         return carry
 
     lax.fori_loop(0, PIECES, drain, 0)
+    lax.fori_loop(0, LAST, drain_results, 0)
+    for copy in extra_moves:
+        for h in range(HEADS):
+            copy(h).wait_send()
     for copy in weight_sends + far_sends:
         copy.wait_send()
     for h in range(HEADS):
@@ -451,9 +511,13 @@
     call = pl.pallas_call(
         kernel,
         out_shape=pltpu.VMEM((rows, width), BF16),
-        in_specs=[hbm] * 5 + [on_chip] * 3,
+        in_specs=[hbm] * 8,
         out_specs=on_chip,
         scratch_shapes=[
+            vmem((HEADS, rows), F32),
+            vmem((1, rows), jnp.int32),
+            vmem(level_weight_table.shape[::-1], F32),
+            dma((3,)),
             vmem((rows, depth), BF16),
             vmem((HEADS, depth, 2 * DH), BF16),
             vmem((depth, width), BF16),
@@ -469,19 +533,19 @@
             vmem((HEADS * CHUNKS, ROWS, 128), F32),
             vmem((HEADS, CTX_Z + 1, MSG, DH), BF16),
             vmem((HEADS, CTX_Z + PLACES_Y - 1, MSG, DH), BF16),
-            vmem((PIECES, HEADS, 4, PIECE, DH), BF16),
+            vmem((PIECES + 1, HEADS, 4, PIECE, DH), BF16),
             vmem((PIECES, HEADS, PIECE, DH), BF16),
             vmem((4, 4, width, width), BF16),
             vmem((4, width, width), BF16),
             vmem((PIECES, 2, PIECE, width), BF16),
             vmem((PIECES, 2, PIECE, width), BF16),
-            vmem((PIECES, 2, PIECE, width), F32),
-            vmem((PIECES, PIECE, width), BF16),
+            vmem((LAST, 2, PIECE, width), F32),
+            vmem((LAST, PIECE, width), BF16),
             dma((CHUNKS,)), dma((5,)), dma((8,)), dma((6,)), dma((6,)),
             dma((HEADS, CTX_Z + PLACES_Y - 1)), dma((HEADS, CTX_Z + PLACES_Y - 1)),
 
-            dma((3, PIECES, HEADS)), dma((3, PIECES, HEADS)),
-            dma((PIECES,)), dma((PIECES,)), dma((PIECES,)), dma((PIECES,)),
+            dma((3, PIECES, HEADS)), dma((3, PIECES, HEADS)), dma((3, HEADS)), dma((3, HEADS)),
+            dma((PIECES,)), dma((PIECES,)), dma((LAST,)), dma((LAST,)),
         ],
         compiler_params=pltpu.CompilerParams(
             collective_id=0, has_side_effects=True, vmem_limit_bytes=56 * 2**20

time: 63.6 us -> 62.1 us (0.976)
  Pallas kernels: 62.5 us -> 61.1 us
    pallas_call x1, Pallas kernels: 62.5 us -> 61.1 us  [shards(): call(tokens, w_query, w_key, w_value, w_out, decay_rate.T, level_row_inde...]
where the time goes in v3:
time: 62.1 us; the launch traced here: 62 us
  Pallas kernels  61.1 us (98%)
  local copies, waits for them, and re-layouts  0.97 us (2%)
    pallas_call x1, Pallas kernels, shards(): call(tokens, w_query, w_key, w_value, w_out, decay_rate.T, level_row_inde...  61.1 us

profile of v3, /device:TPU:1, one launch (start us, length us, event | category | flops | bytes accessed | tf_op | source)
XLA Modules:
  0.0 62.0 jit_solution(11334903771471167609)
XLA Ops:
  0.0 61.1 %shard_map.82 = bf16[2048,256]{1,0:T(8,128)(2,1)S(1)} custom-call(bf16[2048,2048]{1,0:T(8,128)(2,1)} %tokens.1, bf16[2048,256]{1,0:T(8,128)(2,1)} %w_query.1, bf16[2048,256]{1,0:T(8,128)(2,1)} %w_key.1, bf16[2048,256]{1,0:T(8,128)(2,1)} %w_value.1, bf16[256,2048]{1,0:T(8,128)(2,1)} %w_out.1, f32[2,2048]{1,0:T(2,128)} %bitcast.3, s32[1,2048]{1,0:T(1,128)} %bitcast.5, ...), custom_call_target="tpu_custom_call" | custom-call | tf_op jit(solution)/shard_map/pallas_call | solution.py:554
  61.1 1.0 %copy.10 = bf16[2048,256]{1,0:T(8,128)(2,1)} copy(bf16[2048,256]{1,0:T(8,128)(2,1)S(1)} %shard_map.82) | data formatting | bytes 2097152

commit v4 on v3

--- a/solution.py
+++ b/solution.py
@@ -396,8 +396,8 @@
         if h == 1:
             own_to_pair(LAST, h).start()
 
+    receive_z(1, 2)
     receive_y(0)
-    receive_z(1, 2)
     finish(0)
     receive_y(1)
     finish(1)

time: 62.1 us -> 61.9 us (level)
  no operation moved by 1% of the time
where the time goes in v4:
time: 61.9 us; the launch traced here: 61.8 us
  Pallas kernels  60.8 us (98%)
  local copies, waits for them, and re-layouts  0.97 us (2%)
    pallas_call x1, Pallas kernels, shards(): call(tokens, w_query, w_key, w_value, w_out, decay_rate.T, level_row_inde...  60.8 us

profile of v4, /device:TPU:1, one launch (start us, length us, event | category | flops | bytes accessed | tf_op | source)
XLA Modules:
  0.0 61.8 jit_solution(4030391844237631399)
XLA Ops:
  0.0 60.8 %shard_map.82 = bf16[2048,256]{1,0:T(8,128)(2,1)S(1)} custom-call(bf16[2048,2048]{1,0:T(8,128)(2,1)} %tokens.1, bf16[2048,256]{1,0:T(8,128)(2,1)} %w_query.1, bf16[2048,256]{1,0:T(8,128)(2,1)} %w_key.1, bf16[2048,256]{1,0:T(8,128)(2,1)} %w_value.1, bf16[256,2048]{1,0:T(8,128)(2,1)} %w_out.1, f32[2,2048]{1,0:T(2,128)} %bitcast.3, s32[1,2048]{1,0:T(1,128)} %bitcast.5, ...), custom_call_target="tpu_custom_call" | custom-call | tf_op jit(solution)/shard_map/pallas_call | solution.py:554
  60.9 1.0 %copy.10 = bf16[2048,256]{1,0:T(8,128)(2,1)} copy(bf16[2048,256]{1,0:T(8,128)(2,1)S(1)} %shard_map.82) | data formatting | bytes 2097152
